TPU v7x, 128 devices: a whole 4x4x4 slice. The times are simulated.
128 devices in a mesh: dp: 16 (over y, z), cent: 8 (over x, core).
Axes of the slice: x: 4, y: 4, z: 4, core: 2. Of those that a mesh axis runs over, the one named last changes fastest.
Arguments:
- points: bfloat16 [65536, 1024], P(('dp', 'cent')), may hold values from -10 to 10
- candidates: int32 [1024, 2], P(('dp', 'cent')), may hold values from 0 to 15, all different within a row; in each aligned block of 8 rows (0 to 7, 8 to 15, ...) at most 2 rows name the same one
- level_one: bfloat16 [32768, 1024], P(('dp', 'cent')), may hold values from -6 to 6
- level_two: bfloat16 [2048, 1024], P(('dp', 'cent')), may hold values from -6 to 6
Outputs:
- level_one_next: float32 [32768, 1024], P(('dp', 'cent'))
- level_two_next: float32 [2048, 1024], P(('dp', 'cent'))
Inputs may be any that keep to these rules, and one draw needn't show every extreme that they name: `candidates`: among the 8 rows of one device no group is named more than 2 times, and in every draw some device names some group exactly 2 times; the two groups of a row differ.
All inputs are finite; a program needn't handle non-finite values.
Results may differ from a plain program's by a relative error of at most 0.0004.
Values may be sent and summed in bfloat16 or wider, within the bound.
A program may use at most 128 MiB of HBM per device.

v0:
```python
import jax
import jax.numpy as jnp
from jax import lax
from jax.sharding import PartitionSpec as P

CAP = 2


prior_mass = 1.0


def rows_times(left, right):
    return lax.dot_general(
        left, right, (((1,), (1,)), ((), ())), preferred_element_type=jnp.float32
    )


def columns_times(left, right):
    return lax.dot_general(
        left, right, (((0,), (0,)), ((), ())), preferred_element_type=jnp.float32
    )


def local(points, candidates, level_one, level_two):
    groups = lax.axis_size("dp")
    feature_dim = points.shape[1]
    blocks = candidates.shape[0]
    block_rows = points.shape[0] // blocks
    slot_count = groups * CAP
    temp_one = feature_dim / 16.0
    temp_two = feature_dim / 64.0
    highest = lax.Precision.HIGHEST
    targets = candidates.reshape(-1)
    pair_count = targets.shape[0]
    position = jnp.arange(pair_count, dtype=jnp.int32)
    earlier = (targets[None, :] == targets[:, None]) & (position[None, :] < position[:, None])
    ranking = jnp.sum(earlier.astype(jnp.int32), 1)
    slot_of = targets * CAP + ranking
    slot_table = (slot_of[None, :] == jnp.arange(slot_count, dtype=jnp.int32)[:, None]).astype(
        jnp.float32
    )
    pair_owner = (position[:, None] // 2 == jnp.arange(blocks, dtype=jnp.int32)[None, :]).astype(
        jnp.float32
    )
    routing = jnp.dot(slot_table, pair_owner, precision=highest)
    flat_points = points.reshape(blocks, block_rows * feature_dim)
    outgoing = jnp.dot(
        routing.astype(jnp.bfloat16), flat_points, preferred_element_type=jnp.float32
    )
    outgoing = outgoing.astype(jnp.bfloat16).reshape(groups, CAP, block_rows, feature_dim)
    occupied = jnp.sum(slot_table, 1).reshape(groups, CAP).astype(jnp.bfloat16)
    received, occupied_in = (
        lax.all_to_all(outgoing, "dp", split_axis=0, concat_axis=0, tiled=True),
        lax.all_to_all(occupied, "dp", split_axis=0, concat_axis=0, tiled=True),
    )
    centre_block = lax.all_gather(level_one, "cent", axis=0, tiled=True)
    squares = jnp.sum(jnp.square(centre_block.astype(jnp.float32)), 1)
    row_total = groups * CAP * block_rows
    incoming = received.reshape(row_total, feature_dim)
    valid_rows = jnp.repeat(occupied_in.astype(jnp.float32).reshape(-1), block_rows)
    row_step = min(512, row_total)
    step_count = row_total // row_step
    incoming_steps = incoming.reshape(step_count, row_step, feature_dim)

    def scores_of(row_block):
        return (2.0 * rows_times(row_block, centre_block) - squares[None, :]) / temp_one

    def first_stored(row_block):
        block_scores = scores_of(row_block)
        row_peak = jnp.max(block_scores, 1)
        exp_total = jnp.sum(jnp.exp(block_scores - row_peak[:, None]), 1)
        return (block_scores, row_peak, exp_total)

    kept_scores, row_peak, exp_total = lax.map(first_stored, incoming_steps)
    back_peak, back_total = (
        lax.all_to_all(
            row_peak.reshape(groups, CAP, block_rows), "dp", split_axis=0, concat_axis=0, tiled=True
        ),
        lax.all_to_all(
            exp_total.reshape(groups, CAP, block_rows),
            "dp",
            split_axis=0,
            concat_axis=0,
            tiled=True,
        ),
    )
    pair_peak = jnp.einsum(
        "sp,sr->pr", slot_table, back_peak.reshape(slot_count, block_rows), precision=highest
    ).reshape(blocks, 2, block_rows)
    pair_total = jnp.einsum(
        "sp,sr->pr", slot_table, back_total.reshape(slot_count, block_rows), precision=highest
    ).reshape(blocks, 2, block_rows)
    best_peak = jnp.max(pair_peak, 1)
    merged = jnp.sum(pair_total * jnp.exp(pair_peak - best_peak[:, None, :]), 1)
    log_total = best_peak + jnp.log(merged)
    slot_lse = jnp.dot(routing, log_total, precision=highest).reshape(groups, CAP, block_rows)
    lse_in = lax.all_to_all(slot_lse, "dp", split_axis=0, concat_axis=0, tiled=True)
    lse_rows = lse_in.reshape(row_total)
    all_scores = kept_scores.reshape(row_total, -1)
    weights = jnp.where(
        valid_rows[:, None] > 0.0, jnp.exp(all_scores - lse_rows[:, None]), 0.0
    ).astype(jnp.bfloat16)
    group_sums = columns_times(weights, incoming)
    group_mass = jnp.sum(weights.astype(jnp.float32), 0)
    own_sums, own_mass = (
        lax.psum_scatter(group_sums, "cent", scatter_dimension=0, tiled=True),
        lax.psum_scatter(group_mass, "cent", scatter_dimension=0, tiled=True),
    )
    level_one_next = (own_sums + prior_mass * level_one.astype(jnp.float32)) / (
        own_mass[:, None] + prior_mass
    )
    top_block = lax.all_gather(level_two, ("dp", "cent"), axis=0, tiled=True).astype(jnp.float32)
    top_squares = jnp.sum(jnp.square(top_block), 1)
    top_products = lax.dot_general(
        level_one_next,
        top_block,
        (((1,), (1,)), ((), ())),
        precision=highest,
        preferred_element_type=jnp.float32,
    )
    top_scores = (2.0 * top_products - top_squares[None, :]) / temp_two
    top_weights = jax.nn.softmax(top_scores, axis=1)
    top_sums = lax.dot_general(
        top_weights,
        level_one_next,
        (((0,), (0,)), ((), ())),
        precision=highest,
        preferred_element_type=jnp.float32,
    )
    top_mass = jnp.sum(top_weights, 0)
    own_rows = level_two.shape[0]
    total_sums, total_mass = lax.psum((top_sums, top_mass), ("dp", "cent"))
    device_index = lax.axis_index("dp") * lax.axis_size("cent") + lax.axis_index("cent")
    first_row = device_index * own_rows
    share_sums = lax.dynamic_slice_in_dim(total_sums, first_row, own_rows, 0)
    share_mass = lax.dynamic_slice_in_dim(total_mass, first_row, own_rows, 0)
    level_two_next = (share_sums + prior_mass * level_two.astype(jnp.float32)) / (
        share_mass[:, None] + prior_mass
    )
    return (level_one_next, level_two_next)


def solution(mesh):
    placed = (
        P(("dp", "cent"), None),
        P(("dp", "cent"), None),
        P(("dp", "cent"), None),
        P(("dp", "cent"), None),
    )
    return jax.shard_map(
        local,
        mesh=mesh,
        in_specs=placed,
        out_specs=(P(("dp", "cent"), None), P(("dp", "cent"), None)),
        check_vma=False,
    )
```

profile of v0, /device:TPU:0, one launch (start us, length us, event | category | flops | bytes accessed | tf_op | source)
XLA Modules:
  0.0 460.0 jit_solution(14334410055170243211)
XLA Ops:
  12.2 4.3 copy.20
  16.4 8.2 %all-to-all-start.1 = ((bf16[16,2,64,1024]{3,2,1,0:T(8,128)(2,1)}), bf16[16,2,64,1024]{3,2,1,0:T(8,128)(2,1)}, u32[]{:S(2)}, u32[]{:S(2)}) async-start(bf16[16,2,64,1024]{3,2,1,0:T(8,128)(2,1)} %bitcast.49), calls=%async_computation.1 | async-start | bytes 8388608 | tf_op jit(solution)/shard_map/all_to_all | solution.py:53
  25.5 18.8 %all-gather.3.cloned.1.call-done = bf16[2048,1024]{1,0:T(8,128)(2,1)} async-done(((bf16[256,1024]{1,0:T(8,128)(2,1)}), bf16[2048,1024]{1,0:T(8,128)(2,1)}) %all-gather.3.cloned.1.call-update) | async-done | bytes 4194320 | tf_op jit(solution)/shard_map/all_gather | solution.py:56
  44.3 3.1 multiply_reduce_fusion.1
  47.4 39.7 %all-to-all-done.1 = bf16[16,2,64,1024]{3,2,1,0:T(8,128)(2,1)} async-done(((bf16[16,2,64,1024]{3,2,1,0:T(8,128)(2,1)}), bf16[16,2,64,1024]{3,2,1,0:T(8,128)(2,1)}, u32[]{:S(2)}, u32[]{:S(2)}) %all-to-all-start.1) | async-done | bytes 4194336 | tf_op jit(solution)/shard_map/all_to_all | solution.py:53
  87.0 7.8 %broadcast_in_dim.29 = f32[4,512,2048]{2,1,0:T(8,128)} broadcast(f32[]{:T(128)} %constant.32.clone.1), dimensions={} | broadcast | bytes 16777220 | tf_op jit(solution)/shard_map/broadcast_in_dim | solution.py:74
  94.9 55.1 %while.14 = (s32[]{:T(128)}, f32[4,512,2048]{2,1,0:T(8,128)}, f32[4,512]{1,0:T(4,128)S(1)}, f32[4,512]{1,0:T(4,128)S(1)}, bf16[4,512,1024]{2,1,0:T(8,128)(2,1)},...) while((s32[]{:T(128)}, f32[4,512,2048]{2,1,0:T(8,128)}, ...), condition=%wide.region_6.7_spmd, body=%wide.region_3.6_spmd.sunk | while | flops 2153774080 | bytes 22043760 | solution.py:74
  94.9 8.1 %bitcast_dynamic-update-slice_fusion.2 = (f32[4,512,2048]{2,1,0:T(8,128)}, f32[512,2048]{1,0:T(8,128)}) fusion(f32[4,512,2048]{2,1,0:T(8,128)} %get-tuple-element.126, s32[]{:T(128)} %get-tuple-element.125, f32[2048]{0:T(1024)S(1)} %get-tuple-element.141, bf16[2048,1024]{1,0:T(8,128)(2,1)} %get-tuple-element.140, ...), kind=kOutput, calls=%fused_computation.clone.1 | convolution fusion | flops 2150629376 | bytes 13640704 | tf_op jit(solution)/shard_map/while/body/eval_jaxpr/dot_general | solution.py:13
  105.5 2.9 exponential_reduce_fusion.2
  108.5 8.1 %bitcast_dynamic-update-slice_fusion.2 = (f32[4,512,2048]{2,1,0:T(8,128)}, f32[512,2048]{1,0:T(8,128)}) fusion(f32[4,512,2048]{2,1,0:T(8,128)} %get-tuple-element.126, s32[]{:T(128)} %get-tuple-element.125, f32[2048]{0:T(1024)S(1)} %get-tuple-element.141, bf16[2048,1024]{1,0:T(8,128)(2,1)} %get-tuple-element.140, ...), kind=kOutput, calls=%fused_computation.clone.1 | convolution fusion | flops 2150629376 | bytes 13640704 | tf_op jit(solution)/shard_map/while/body/eval_jaxpr/dot_general | solution.py:13
  119.3 2.9 exponential_reduce_fusion.2
  122.4 8.5 %bitcast_dynamic-update-slice_fusion.2 = (f32[4,512,2048]{2,1,0:T(8,128)}, f32[512,2048]{1,0:T(8,128)}) fusion(f32[4,512,2048]{2,1,0:T(8,128)} %get-tuple-element.126, s32[]{:T(128)} %get-tuple-element.125, f32[2048]{0:T(1024)S(1)} %get-tuple-element.141, bf16[2048,1024]{1,0:T(8,128)(2,1)} %get-tuple-element.140, ...), kind=kOutput, calls=%fused_computation.clone.1 | convolution fusion | flops 2150629376 | bytes 13640704 | tf_op jit(solution)/shard_map/while/body/eval_jaxpr/dot_general | solution.py:13
  133.4 2.9 exponential_reduce_fusion.2
  136.4 8.2 %bitcast_dynamic-update-slice_fusion.2 = (f32[4,512,2048]{2,1,0:T(8,128)}, f32[512,2048]{1,0:T(8,128)}) fusion(f32[4,512,2048]{2,1,0:T(8,128)} %get-tuple-element.126, s32[]{:T(128)} %get-tuple-element.125, f32[2048]{0:T(1024)S(1)} %get-tuple-element.141, bf16[2048,1024]{1,0:T(8,128)(2,1)} %get-tuple-element.140, ...), kind=kOutput, calls=%fused_computation.clone.1 | convolution fusion | flops 2150629376 | bytes 13640704 | tf_op jit(solution)/shard_map/while/body/eval_jaxpr/dot_general | solution.py:13
  147.0 2.9 exponential_reduce_fusion.2
  150.8 10.3 %all-to-all-start.2 = ((f32[16,1,128]{2,1,0:T(1,128)}), f32[16,1,128]{2,1,0:T(1,128)S(1)}, u32[]{:S(2)}, u32[]{:S(2)}) async-start(f32[16,1,128]{2,1,0:T(1,128)} %reshape.180), calls=%async_computation.2 | async-start | bytes 16384 | tf_op jit(solution)/shard_map/all_to_all | solution.py:76
  161.9 6.7 %all-to-all-done.2 = f32[16,1,128]{2,1,0:T(1,128)S(1)} async-done(((f32[16,1,128]{2,1,0:T(1,128)}), f32[16,1,128]{2,1,0:T(1,128)S(1)}, u32[]{:S(2)}, u32[]{:S(2)}) %all-to-all-start.2) | async-done | bytes 8224 | tf_op jit(solution)/shard_map/all_to_all | solution.py:76
  168.6 3.5 all-to-all-start.3
  174.1 5.4 %all-to-all-done.3 = f32[16,1,128]{2,1,0:T(1,128)S(1)} async-done(((f32[16,1,128]{2,1,0:T(1,128)}), f32[16,1,128]{2,1,0:T(1,128)S(1)}, u32[]{:S(2)}, u32[]{:S(2)}) %all-to-all-start.3) | async-done | bytes 8224 | tf_op jit(solution)/shard_map/all_to_all | solution.py:79
  179.5 3.4 all-to-all-start
  184.9 5.5 %all-to-all-done = bf16[16,1,2]{2,1,0:T(2,128)(2,1)S(1)} async-done(((bf16[16,1,2]{2,1,0:T(2,128)(2,1)}), bf16[16,1,2]{2,1,0:T(2,128)(2,1)S(1)}, u32[]{:S(2)}, u32[]{:S(2)}) %all-to-all-start) | async-done | bytes 96 | tf_op jit(solution)/shard_map/all_to_all | solution.py:54
  190.4 3.5 all-to-all-start.4
  194.4 6.9 %all-to-all-done.4 = f32[16,1,128]{2,1,0:T(1,128)S(1)} async-done(((f32[16,1,128]{2,1,0:T(1,128)}), f32[16,1,128]{2,1,0:T(1,128)S(1)}, u32[]{:S(2)}, u32[]{:S(2)}) %all-to-all-start.4) | async-done | bytes 8224 | tf_op jit(solution)/shard_map/all_to_all | solution.py:97
  202.0 7.7 %convert_reduce_fusion = (f32[2048]{0:T(1024)S(1)}, bf16[4,512,2048]{2,1,0:T(8,128)(2,1)S(1)}) fusion(f32[4,512,2048]{2,1,0:T(8,128)} %get-tuple-element.41, f32[4,512]{1,0:T(4,128)S(1)} %sub.59, pred[4,512]{1,0:T(4,128)(4,1)S(1)} %gt.23), kind=kLoop, calls=%fused_computation.7 | loop fusion | flops 20969472 | bytes 25184256 | tf_op jit(solution)/shard_map/reduce_sum | solution.py:104
  209.7 13.2 %fusion.27 = f32[2048,1024]{1,0:T(8,128)} fusion(bf16[2048,2048]{1,0:T(8,128)(2,1)S(1)} %bitcast.51, bf16[2048,1024]{1,0:T(8,128)(2,1)} %bitcast.12), kind=kOutput, calls=%fused_computation.52 | convolution fusion | flops 8589934592 | bytes 20971520 | tf_op jit(solution)/shard_map/dot_general | solution.py:19
  224.8 12.8 %all-reduce = f32[2048]{0:T(1024)S(1)} all-reduce(f32[2048]{0:T(1024)S(1)} %get-tuple-element.58), channel_id=3, replica_groups=mesh['dp'=16,'cent'=8] {'cent'}, use_global_device_ids=true, to_apply=%region_11.12.clone | all-reduce | flops 2048 | bytes 16384
  237.7 3.1 multiply_reduce_fusion
  240.9 32.2 %reduce-scatter.2.cloned.1.call-done = f32[256,1024]{1,0:T(8,128)} async-done(((f32[2048,1024]{1,0:T(8,128)}), f32[256,1024]{1,0:T(8,128)}) %reduce-scatter.2.cloned.1.call-update) | async-done | bytes 1048592 | tf_op jit(solution)/shard_map/reduce_scatter | solution.py:106
  274.6 5.9 %fusion.26 = (f32[256]{0:T(256)S(1)}, f32[256,2048]{1,0:T(8,128)S(1)}) fusion(f32[2048]{0:T(1024)S(1)} %multiply_reduce_fusion, f32[256,1024]{1,0:T(8,128)S(1)} %add_divide_fusion, bf16[2048,1024]{1,0:T(8,128)(2,1)} %all-gather.5.cloned.1.call-done), kind=kOutput, calls=%fused_computation.51 | convolution fusion | flops 6444548096 | bytes 7349248 | tf_op jit(solution)/shard_map/dot_general | solution.py:114
  280.9 9.3 %fusion.23 = f32[2048,1024]{1,0:T(8,128)} fusion(f32[256,1024]{1,0:T(8,128)S(1)} %add_divide_fusion, f32[256,2048]{1,0:T(8,128)S(1)} %get-tuple-element.65, f32[256]{0:T(256)S(1)} %fusion.6, f32[256]{0:T(256)S(1)} %get-tuple-element.64), kind=kOutput, calls=%fused_computation.49 | convolution fusion | flops 6443499520 | bytes 11536384 | tf_op jit(solution)/shard_map/dot_general | solution.py:123
  290.8 65.2 %psum.15 = f32[2048]{0:T(1024)S(1)} all-reduce(f32[2048]{0:T(1024)S(1)} %fusion.22), channel_id=1, replica_groups=mesh['dp'=16,'cent'=8] {'dp','cent'}, use_global_device_ids=true, to_apply=%region_17.18 | all-reduce | flops 2048 | bytes 16384 | tf_op jit(solution)/shard_map/psum | solution.py:132
  356.1 95.8 %all-reduce.3.cloned.1.call-done = f32[2048,1024]{1,0:T(8,128)} async-done(((f32[2048,1024]{1,0:T(8,128)}), f32[2048,1024]{1,0:T(8,128)}) %all-reduce.3.cloned.1.call-update) | async-done | bytes 8388624 | tf_op jit(solution)/shard_map/psum | solution.py:132
  (70 shorter events, 28.4 us)
Async XLA Ops:
  7.2 37.1 %all-gather.3.cloned.1.call-start = ((), (), s32[]{:S(2)}) async-start(), calls=%async_computation.6 | async-start | bytes 4718592 | tf_op jit(solution)/shard_map/all_gather | solution.py:56
  16.4 70.6 %all-to-all-start.1 = ((bf16[16,2,64,1024]{3,2,1,0:T(8,128)(2,1)}), bf16[16,2,64,1024]{3,2,1,0:T(8,128)(2,1)}, u32[]{:S(2)}, u32[]{:S(2)}) async-start(bf16[16,2,64,1024]{3,2,1,0:T(8,128)(2,1)} %bitcast.49), calls=%async_computation.1 | async-start | bytes 8388608 | tf_op jit(solution)/shard_map/all_to_all | solution.py:53
  24.6 213.1 %all-gather.5.cloned.1.call-start = ((), (), s32[]{:S(2)}) async-start(), calls=%async_computation.8 | async-start | bytes 4227072 | tf_op jit(solution)/shard_map/all_gather | solution.py:112
  150.8 17.8 %all-to-all-start.2 = ((f32[16,1,128]{2,1,0:T(1,128)}), f32[16,1,128]{2,1,0:T(1,128)S(1)}, u32[]{:S(2)}, u32[]{:S(2)}) async-start(f32[16,1,128]{2,1,0:T(1,128)} %reshape.180), calls=%async_computation.2 | async-start | bytes 16384 | tf_op jit(solution)/shard_map/all_to_all | solution.py:76
  168.6 10.9 %all-to-all-start.3 = ((f32[16,1,128]{2,1,0:T(1,128)}), f32[16,1,128]{2,1,0:T(1,128)S(1)}, u32[]{:S(2)}, u32[]{:S(2)}) async-start(f32[16,1,128]{2,1,0:T(1,128)} %reshape.182), calls=%async_computation.3 | async-start | bytes 16384 | tf_op jit(solution)/shard_map/all_to_all | solution.py:79
  179.5 10.9 %all-to-all-start = ((bf16[16,1,2]{2,1,0:T(2,128)(2,1)}), bf16[16,1,2]{2,1,0:T(2,128)(2,1)S(1)}, u32[]{:S(2)}, u32[]{:S(2)}) async-start(bf16[16,1,2]{2,1,0:T(2,128)(2,1)} %convert_element_type.69), calls=%async_computation | async-start | bytes 16384 | tf_op jit(solution)/shard_map/all_to_all | solution.py:54
  190.4 10.9 %all-to-all-start.4 = ((f32[16,1,128]{2,1,0:T(1,128)}), f32[16,1,128]{2,1,0:T(1,128)S(1)}, u32[]{:S(2)}, u32[]{:S(2)}) async-start(f32[16,1,128]{2,1,0:T(1,128)} %reshape.184), calls=%async_computation.4 | async-start | bytes 16384 | tf_op jit(solution)/shard_map/all_to_all | solution.py:97
  193.9 79.3 %reduce-scatter.2.cloned.1.call-start = ((), (), s32[]{:S(2)}) async-start(), calls=%async_computation.7 | async-start | bytes 9437184 | tf_op jit(solution)/shard_map/reduce_scatter | solution.py:106
  222.9 0.7 copy-start.3
  223.0 50.2 %copy-start.1 = (bf16[256,1024]{1,0:T(8,128)(2,1)S(1)}, bf16[256,1024]{1,0:T(8,128)(2,1)}, u32[]{:S(2)}) copy-start(bf16[256,1024]{1,0:T(8,128)(2,1)} %param.8) | copy-start | bytes 1572868
  223.0 229.0 %all-reduce.3.cloned.1.call-start = ((), (), s32[]{:S(2)}) async-start(), calls=%async_computation.9 | async-start | bytes 16777216 | tf_op jit(solution)/shard_map/psum | solution.py:132
  274.5 6.3 %copy-start = (f32[256,1024]{1,0:T(8,128)}, f32[256,1024]{1,0:T(8,128)S(1)}, u32[]{:S(2)}) copy-start(f32[256,1024]{1,0:T(8,128)S(1)} %add_divide_fusion) | copy-start | bytes 3145732
  290.2 161.8 %copy-start.2 = (bf16[16,1024]{1,0:T(8,128)(2,1)S(1)}, bf16[16,1024]{1,0:T(8,128)(2,1)}, u32[]{:S(2)}) copy-start(bf16[16,1024]{1,0:T(8,128)(2,1)} %param.9) | copy-start | bytes 98308
Sparse Core Ops, SparseCore 0:
  9.7 34.5 all-gather.2
  47.4 81.9 all-gather.4
  223.1 50.0 reduce-scatter.1
  290.3 161.5 all-reduce.2
where the time goes:
time: 462 us; the launch traced here: 460 us
  waiting for transfers between devices  212 us (46%)
  blocking collectives  78 us (17%)
  matrix products  63.5 us (14%)
  other arithmetic  41.7 us (9%)
  starting transfers between devices  29.2 us (6%)
  local copies, waits for them, and re-layouts  20.4 us (4%)
  between operations  14.6 us (3%)
    psum x1, waiting for transfers between devices, local(): total_sums, total_mass = lax.psum((top_sums, top_mass), ('dp', 'cent'))  95.8 us
    psum x1, blocking collectives, local(): total_sums, total_mass = lax.psum((top_sums, top_mass), ('dp', 'cent'))  65.2 us
    all_to_all x1, waiting for transfers between devices, local(): lax.all_to_all(outgoing, 'dp', split_axis=0, concat_axis=0, tiled=True)  39.7 us
    dot_general x4, matrix products, rows_times(): lax.dot_general(left, right, (((1,), (1,)), ((), ())), preferred_element_...  33 us
    reduce_scatter x1, waiting for transfers between devices, local(): lax.psum_scatter(group_sums, 'cent', scatter_dimension=0, tiled=True)  32.2 us
    all_gather x1, waiting for transfers between devices, local(): centre_block = lax.all_gather(level_one, 'cent', axis=0, tiled=True)  18.8 us
    dot_general x1, matrix products, columns_times(): lax.dot_general(left, right, (((0,), (0,)), ((), ())), preferred_element_...  13.2 us
    unnamed x1, blocking collectives  12.8 us
  transfers between devices with their start and end apart: 9, of which 8 were waited for; matrix products, arithmetic and copies ran while one was open for 23% of the time, Pallas kernels for 0%

commit v1 on v0

v1 whole, which is shorter than its diff:
```python
import functools

import jax
import jax.numpy as jnp
from jax import lax
from jax.experimental import pallas as pl
from jax.experimental.pallas import tpu as pltpu
from jax.sharding import PartitionSpec as P

MESH = pl.DeviceIdType.MESH
CAP = 2
PRIOR = 1.0
BIG = 1e5
F32 = jnp.float32
BF16 = jnp.bfloat16
PEERS = [(dy, dz) for dy in range(4) for dz in range(4) if (dy, dz) != (0, 0)]
NEAR = [(dy, dz) for dy in (0, 1, 3) for dz in (0, 1, 3)]
FAR = [(2, 0), (2, 1), (2, 2), (2, 3), (0, 2), (1, 2), (3, 2)]
AXES_OF = ((2, 1, 0), (1, 0, 2), (0, 2, 1))


def nt(left, right):
    return lax.dot_general(
        left, right, (((1,), (1,)), ((), ())), preferred_element_type=F32
    )


def nn(left, right):
    return jnp.dot(left, right, preferred_element_type=F32)


def log_add(a, b):
    top = jnp.maximum(a, b)
    return top + jnp.log(jnp.exp(a - top) + jnp.exp(b - top))


def source_of(i):
    j = i - 9
    near_y, near_z = i // 3, i % 3
    far_t = j - 4
    dy = jnp.where(
        i < 9, near_y + near_y // 2, jnp.where(j < 4, 2, far_t + far_t // 2)
    )
    dz = jnp.where(i < 9, near_z + near_z // 2, jnp.where(j < 4, j, 2))
    return dy, dz


def step_kernel(
    pts, cen, table, zin,
    one_out, two_out,
    tt, tt_sib, tts, zg1, zg2, zg3, yg1, yg2, yg3, outz, outy, x_all, c_all, sq, scores,
    st, sto, stc, g_all, lse, w_buf, sums, sum_half, sum_full,
    mass, mass_in, z_all, zsq, ch, stat, stat_in, wh, wl,
    ha0, fu0, ha1, fu1, ha2, fu2,
    ssem, rsem, lsem,
):
    dp = lax.axis_index("dp")
    cent = lax.axis_index("cent")
    y, z = dp // 4, dp % 4
    x, c = cent // 2, cent % 2
    zg = (None, zg1, zg2, zg3)
    yg = (None, yg1, yg2, yg3)

    def at(dy=0, dz=0, dx=0, dc=0):
        return (
            ((y + dy) % 4) * 4 + (z + dz) % 4,
            ((x + dx) % 4) * 2 + (c + dc) % 2,
        )

    def along(axis, d):
        return at(*[d if a == axis else 0 for a in range(3)])

    sent = []
    counter = [0]

    def send(src, dst, device):
        n = counter[0]
        counter[0] += 1
        copy = pltpu.make_async_remote_copy(
            src_ref=src,
            dst_ref=dst,
            send_sem=ssem.at[n],
            recv_sem=rsem.at[n],
            device_id=device,
            device_id_type=MESH,
        )
        copy.start()
        sent.append(copy)
        return copy

    barrier = pltpu.get_barrier_semaphore()
    friends = [dict(dy=a, dz=b) for a, b in PEERS]
    friends += [dict(dc=1), dict(dx=1), dict(dx=2), dict(dx=3)]
    for f in friends:
        pl.semaphore_signal(barrier, inc=1, device_id=at(**f), device_id_type=MESH)
    pl.semaphore_wait(barrier, len(friends))

    z_one = {d: send(pts.at[:, 0], zg[d], along(1, d)) for d in (1, 3)}
    y_one = {d: send(pts.at[:, 1], yg[d], along(0, d)) for d in (1, 3)}
    c_one = {d: send(cen, c_all.at[d], along(2, d)) for d in (1, 3)}
    t_copy = {
        (a, b): send(table, tt.at[dp], at(dy=a, dz=b)) for a, b in PEERS
    }
    zx = {d: send(zin, z_all.at[0, 0, d], along(2, d)) for d in (1, 2, 3)}
    tt[dp] = table[...]
    c_all[0] = cen[...]
    z_all[0, 0, 0] = zin[...]
    for t in t_copy.values():
        t.wait_recv()
    tt_copy = send(tt, tt_sib, at(dc=1))
    local = pltpu.make_async_copy(tt, tts, lsem.at[0])
    local.start()
    local.wait()

    arrive = {}

    def slots(r):
        from_z = tts.at[y * 4 + (z - r) % 4]
        from_y = tts.at[((y - r) % 4) * 4 + z]
        for d in (2, 1, 3, 0):
            for k in range(2):
                group = ((y + d) % 4) * 4 + z
                pick = from_z[0, group * CAP + k]
                block = pts[pick, 0] if r == 0 else zg[r][pick]
                if d == 0:
                    x_all[r, k, c, 0] = block
                else:
                    outz[r, d - 1, k] = block
                group = y * 4 + (z + d) % 4
                pick = from_y[0, group * CAP + k]
                block = pts[pick, 1] if r == 0 else yg[r][pick]
                if d == 0:
                    x_all[r * 4, k, c, 1] = block
                else:
                    outy[r, d - 1, k] = block
            if d != 0:
                arrive[d, r, 0] = send(
                    outz.at[r, d - 1], x_all.at[d * 4 + r, :, c, 0], along(0, d)
                )
                arrive[r, d, 1] = send(
                    outy.at[r, d - 1], x_all.at[r * 4 + d, :, c, 1], along(1, d)
                )

    slots(0)
    z_one[1].wait_recv()
    z_fwd = [send(zg[1].at[0:4], zg[2].at[0:4], along(1, 1))]
    y_one[1].wait_recv()
    y_fwd = [send(yg[1].at[0:4], yg[2].at[0:4], along(0, 1))]
    z_one[3].wait_recv()
    z_fwd.append(send(zg[3].at[4:8], zg[2].at[4:8], along(1, 3)))
    y_one[3].wait_recv()
    y_fwd.append(send(yg[3].at[4:8], yg[2].at[4:8], along(0, 3)))
    c_one[1].wait_recv()
    c_fwd = [send(c_all.at[1, 0:128], c_all.at[2, 0:128], along(2, 1))]
    c_one[3].wait_recv()
    c_fwd.append(send(c_all.at[3, 128:256], c_all.at[2, 128:256], along(2, 3)))
    slots(1)
    slots(3)
    for copy in z_fwd + y_fwd:
        copy.wait_recv()
    slots(2)
    for copy in c_fwd:
        copy.wait_recv()

    centres = c_all[...].reshape(1024, 1024)
    sq[...] = (
        jnp.sum(jnp.square(centres.astype(F32)), 1, keepdims=True) * (1.0 / 64.0)
        + jnp.zeros((1024, 128), F32)
    )

    def score_chunk(i, carry):
        dy, dz = source_of(i)
        s = dy * 4 + dz
        s_abs = ((y - dy) % 4) * 4 + (z - dz) % 4
        rows = x_all[s].reshape(256, 1024)
        product = nt(c_all[...].reshape(1024, 1024), rows)
        for k in range(2):
            half = product[:, k * 128:(k + 1) * 128] * (1.0 / 32.0) - sq[...]
            scores[s * 2 + k] = half.reshape(4, 4, 4, 16, 128)
            peak = jnp.max(half, 0, keepdims=True)
            total = jnp.sum(jnp.exp(half - peak), 0, keepdims=True)
            st[k, pl.ds(s_abs, 1), :] = peak + jnp.log(total)
        return carry

    sib = {}

    def forward(group):
        for dy, dz in group:
            s = dy * 4 + dz
            if dy:
                arrive[dy, dz, 0].wait_recv()
            if dz:
                arrive[dy, dz, 1].wait_recv()
            sib[dy, dz] = send(x_all.at[s, :, c], x_all.at[s, :, c], at(dc=1))

    forward(NEAR)
    for p in NEAR:
        sib[p].wait_recv()
    lax.fori_loop(0, 9, score_chunk, 0)
    forward(FAR)
    for p in FAR:
        sib[p].wait_recv()
    lax.fori_loop(9, 16, score_chunk, 0)

    st_copy = send(st, sto, at(dc=1))
    st_copy.wait_recv()
    stc[...] = log_add(st[...], sto[...])
    g_copies = [send(stc, g_all.at[dp], at(dy=a, dz=b)) for a, b in PEERS]
    g_all[dp] = stc[...]
    for copy in zx.values():
        copy.wait_recv()
    for copy in g_copies:
        copy.wait_recv()
    zz = [send(z_all.at[0, 0], z_all.at[0, d], along(1, d)) for d in (1, 2, 3)]
    tt_copy.wait_recv()
    lane = lax.broadcasted_iota(jnp.int32, (16, 128), 1)
    mine = lane // 64 == c
    wide = lax.broadcasted_iota(jnp.int32, (16, 512), 1).astype(F32)
    source = lax.broadcasted_iota(jnp.int32, (16, 1), 0).astype(F32)
    table_rows = g_all[...].reshape(512, 128)

    def other_group(tables_of, k):
        partner = tables_of[:, 1, :].astype(F32)
        slot = jnp.sum(jnp.where(lane == dp * CAP + k, partner, 0.0), 1, keepdims=True)
        match = (wide == slot * 16.0 + source).astype(F32)
        other = jnp.dot(
            match, table_rows, precision=lax.Precision.HIGHEST, preferred_element_type=F32
        )
        return jnp.where(slot >= 0.0, log_add(stc[k], other), BIG)

    for k in range(2):
        lse[k] = jnp.where(mine, other_group(tt, k), other_group(tt_sib, k))

    def weigh(r):
        def one(s, carry):
            dy, dz = s // 4, s % 4
            s_abs = ((y - dy) % 4) * 4 + (z - dz) % 4
            for k in range(2):
                col = pl.multiple_of(s * 256 + k * 128, 128)
                row = lse[k, pl.ds(s_abs, 1), :]
                w_buf[:, pl.ds(col, 128)] = jnp.exp(
                    scores[s * 2 + k, r].reshape(256, 128) - row
                ).astype(BF16)
            return carry

        lax.fori_loop(0, 16, one, 0)
        mass[r] = nt(jnp.ones((8, 4096), BF16), w_buf[...])

        def tile(n, carry):
            col = pl.multiple_of(n * 256, 256)
            rows = x_all[:, :, :, :, :, pl.ds(col, 256)].reshape(4096, 256)
            sums[r, :, pl.ds(col, 256)] = nn(w_buf[...], rows)
            return carry

        lax.fori_loop(0, 4, tile, 0)

    lo, hi = pl.ds(0, 128), pl.ds(128, 128)
    weigh(2)
    via_a = send(sums.at[2, lo], sum_half.at[0], along(2, 1))
    via_b = send(sums.at[2, hi], sum_half.at[1], along(2, 3))
    mass_a = send(mass.at[2], mass_in.at[0], along(2, 1))
    for copy in zz:
        copy.wait_recv()
    zy = [send(z_all.at[0], z_all.at[d], along(0, d)) for d in (1, 2, 3)]
    weigh(3)
    last = [send(sums.at[3, hi], sum_full.at[0, hi], along(2, 1))]
    weigh(1)
    last.append(send(sums.at[1, lo], sum_full.at[1, lo], along(2, 3)))
    last.append(send(mass.at[1], mass_in.at[2], along(2, 3)))
    via_a.wait_recv()
    sums[3, lo] += sum_half[0]
    last.append(send(sums.at[3, lo], sum_full.at[0, lo], along(2, 1)))
    mass_a.wait_recv()
    mass[3] += mass_in[0]
    last.append(send(mass.at[3], mass_in.at[1], along(2, 1)))
    via_b.wait_recv()
    sums[1, hi] += sum_half[1]
    last.append(send(sums.at[1, hi], sum_full.at[1, hi], along(2, 3)))
    weigh(0)
    for copy in zy:
        copy.wait_recv()
    zsq[...] = (
        jnp.sum(
            jnp.square(z_all[...].reshape(1024, 1024).astype(F32)), 1, keepdims=True
        ) * (1.0 / 16.0)
        + jnp.zeros((1024, 128), F32)
    )
    for copy in last:
        copy.wait_recv()
    own_mass = jnp.transpose(mass[0] + mass_in[1] + mass_in[2])[:, 0:1]
    own_sums = sums[0] + sum_full[0] + sum_full[1]
    one_out[...] = (own_sums + PRIOR * cen[...].astype(F32)) / (own_mass + PRIOR)

    ch[0, 0] = one_out[...].astype(BF16)
    ch[0, 1] = (one_out[...] - ch[0, 0].astype(F32)).astype(BF16)
    ch_copy = send(ch.at[0], ch.at[1], at(dc=1))

    def top_scores(h, carry):
        zs = z_all[...].reshape(1024, 1024)
        product = nt(zs, ch[h, 0]) + nt(zs, ch[h, 1])
        for k in range(2):
            cols = slice(k * 128, (k + 1) * 128)
            half = product[:, cols] * (1.0 / 8.0) - zsq[...]
            scores[16 + h * 2 + k] = half.reshape(4, 4, 4, 16, 128)
            peak = jnp.max(half, 0, keepdims=True)
            stat[h, 0:1, cols] = peak
            stat[h, 1:2, cols] = jnp.sum(jnp.exp(half - peak), 0, keepdims=True)
        return carry

    lax.fori_loop(0, 1, top_scores, 0)
    ch_copy.wait_recv()
    lax.fori_loop(1, 2, top_scores, 0)
    stat_copy = send(stat, stat_in, at(dc=1))
    stat_copy.wait_recv()
    mass_two = jnp.zeros((1024, 1), F32)
    for h in range(2):
        peak = jnp.maximum(stat[h, 0:1], stat_in[1 - h, 0:1])
        total = stat[h, 1:2] * jnp.exp(stat[h, 0:1] - peak) + stat_in[
            1 - h, 1:2
        ] * jnp.exp(stat_in[1 - h, 0:1] - peak)
        scale = 1.0 / total
        for k in range(2):
            part = slice(k * 128, (k + 1) * 128)
            weight = (
                jnp.exp(scores[16 + h * 2 + k].reshape(1024, 128) - peak[:, part])
                * scale[:, part]
            )
            cols = slice(h * 256 + k * 128, h * 256 + (k + 1) * 128)
            wh[:, cols] = weight.astype(BF16)
            wl[:, cols] = (weight - wh[:, cols].astype(F32)).astype(BF16)
            mass_two = mass_two + jnp.sum(weight, 1, keepdims=True)
    for q in range(4):
        cols = slice(q * 256, (q + 1) * 256)
        hi_rows = ch[:, 0, :, cols].reshape(512, 256)
        lo_rows = ch[:, 1, :, cols].reshape(512, 256)
        part = nn(wh[...], hi_rows) + nn(wl[...], hi_rows) + nn(wh[...], lo_rows)
        for k in range(2):
            scores[q * 2 + k] = part[:, k * 128:(k + 1) * 128].reshape(4, 4, 4, 16, 128)
    scores[8] = (mass_two + jnp.zeros((1024, 128), F32)).reshape(4, 4, 4, 16, 128)

    halves = (ha0, ha1, ha2)
    fulls = (fu0, fu1, fu2)

    def chunk(q, stage, r, half=None):
        where = [slice(None)] * 3
        for done in AXES_OF[q][:stage]:
            where[done] = 0
        where[AXES_OF[q][stage]] = r
        if half is not None:
            if stage < 2:
                free = min(AXES_OF[q][stage + 1:])
                where[free] = pl.ds(half * 2, 2)
            else:
                where.append(pl.ds(half * 8, 8))
        return scores.at[(pl.ds(q * 3, 3), *where)]

    def part_of(ref, stage, half):
        size = 2 if stage < 2 else 8
        return ref.at[:, pl.ds(half * size, size)]

    for stage in range(3):
        ha, fu = halves[stage], fulls[stage]
        first, second = {}, {}
        for q in range(3):
            axis = AXES_OF[q][stage]
            first[q] = (
                send(chunk(q, stage, 2, 0), ha.at[q, 0], along(axis, 1)),
                send(chunk(q, stage, 2, 1), ha.at[q, 1], along(axis, 3)),
            )
        for q in range(3):
            axis = AXES_OF[q][stage]
            second[q] = [
                send(chunk(q, stage, 3, 1), part_of(fu.at[q, 0], stage, 1), along(axis, 1)),
                send(chunk(q, stage, 1, 0), part_of(fu.at[q, 1], stage, 0), along(axis, 3)),
            ]
        for q in range(3):
            axis = AXES_OF[q][stage]
            first[q][0].wait_recv()
            view = chunk(q, stage, 3, 0)
            view[...] += ha[q, 0]
            second[q].append(send(view, part_of(fu.at[q, 0], stage, 0), along(axis, 1)))
            first[q][1].wait_recv()
            view = chunk(q, stage, 1, 1)
            view[...] += ha[q, 1]
            second[q].append(send(view, part_of(fu.at[q, 1], stage, 1), along(axis, 3)))
        for q in range(3):
            for copy in second[q]:
                copy.wait_recv()
            view = chunk(q, stage, 0)
            view[...] += fu[q, 0] + fu[q, 1]
    denominator = scores[8, 0, 0, 0, :, 0:1] + PRIOR
    for q in range(8):
        cols = slice(q * 128, (q + 1) * 128)
        two_out[:, cols] = (
            scores[q, 0, 0, 0] + PRIOR * zin[:, cols].astype(F32)
        ) / denominator
    for copy in sent:
        copy.wait_send()


def tables(candidates):
    targets = candidates.reshape(-1)
    count = targets.shape[0]
    position = jnp.arange(count, dtype=jnp.int32)
    earlier = (targets[None, :] == targets[:, None]) & (
        position[None, :] < position[:, None]
    )
    slot = targets * CAP + jnp.sum(earlier.astype(jnp.int32), 1)
    mate = jnp.stack([slot[1::2], slot[0::2]], 1).reshape(-1)
    lanes = jnp.arange(128, dtype=jnp.int32)
    hit = slot[:, None] == lanes[None, :]
    block = jnp.sum(jnp.where(hit, (position // 2)[:, None], 0), 0)
    partner = jnp.sum(jnp.where(hit, mate[:, None] + 1, 0), 0) - 1
    rest = jnp.zeros((6, 128), jnp.int32)
    return jnp.concatenate([block[None], partner[None], rest], 0)


def local(points, candidates, level_one, level_two):
    vmem = pl.BlockSpec(memory_space=pltpu.VMEM)
    n_copies = 158
    dma = pltpu.SemaphoreType.DMA
    scratch = [
        pltpu.VMEM((16, 8, 128), jnp.int32),
        pltpu.VMEM((16, 8, 128), jnp.int32),
        pltpu.SMEM((16, 8, 128), jnp.int32),
        *[pltpu.VMEM((8, 32, 1024), BF16)] * 3,
        *[pltpu.VMEM((8, 32, 1024), BF16)] * 3,
        pltpu.VMEM((4, 3, 2, 32, 1024), BF16),
        pltpu.VMEM((4, 3, 2, 32, 1024), BF16),
        pltpu.VMEM((16, 2, 2, 2, 32, 1024), BF16),
        pltpu.VMEM((4, 256, 1024), BF16),
        pltpu.VMEM((1024, 128), F32),
        pltpu.VMEM((32, 4, 4, 4, 16, 128), F32),
        pltpu.VMEM((2, 16, 128), F32),
        pltpu.VMEM((2, 16, 128), F32),
        pltpu.VMEM((2, 16, 128), F32),
        pltpu.VMEM((16, 2, 16, 128), F32),
        pltpu.VMEM((2, 16, 128), F32),
        pltpu.VMEM((256, 4096), BF16),
        pltpu.VMEM((4, 256, 1024), F32),
        pltpu.VMEM((2, 128, 1024), F32),
        pltpu.VMEM((2, 256, 1024), F32),
        pltpu.VMEM((4, 8, 256), F32),
        pltpu.VMEM((3, 8, 256), F32),
        pltpu.VMEM((4, 4, 4, 16, 1024), BF16),
        pltpu.VMEM((1024, 128), F32),
        pltpu.VMEM((2, 2, 256, 1024), BF16),
        pltpu.VMEM((2, 8, 256), F32),
        pltpu.VMEM((2, 8, 256), F32),
        pltpu.VMEM((1024, 512), BF16),
        pltpu.VMEM((1024, 512), BF16),
        pltpu.VMEM((3, 2, 3, 2, 4, 16, 128), F32),
        pltpu.VMEM((3, 2, 3, 4, 4, 16, 128), F32),
        pltpu.VMEM((3, 2, 3, 2, 16, 128), F32),
        pltpu.VMEM((3, 2, 3, 4, 16, 128), F32),
        pltpu.VMEM((3, 2, 3, 8, 128), F32),
        pltpu.VMEM((3, 2, 3, 16, 128), F32),
        dma((n_copies,)),
        dma((n_copies,)),
        dma((1,)),
    ]
    return pl.pallas_call(
        step_kernel,
        out_shape=(
            jax.ShapeDtypeStruct((256, 1024), F32),
            jax.ShapeDtypeStruct((16, 1024), F32),
        ),
        in_specs=[vmem] * 4,
        out_specs=(vmem, vmem),
        scratch_shapes=scratch,
        compiler_params=pltpu.CompilerParams(
            collective_id=0, has_side_effects=True, vmem_limit_bytes=62 * 2**20
        ),
        name="lloyd_step",
    )(points.reshape(8, 2, 32, 1024), level_one, tables(candidates), level_two)


def solution(mesh):
    placed = P(("dp", "cent"), None)
    return jax.shard_map(
        local,
        mesh=mesh,
        in_specs=(placed,) * 4,
        out_specs=(placed, placed),
        check_vma=False,
    )
```

time: 462 us -> 172 us (0.37)
  waiting for transfers between devices: 212 us -> 0 us
  Pallas kernels: 0 us -> 166 us
  blocking collectives: 78 us -> 0 us
  matrix products: 63.5 us -> 0 us
  other arithmetic: 41.7 us -> 0.97 us
  starting transfers between devices: 29.2 us -> 0 us
  local copies, waits for them, and re-layouts: 20.4 us -> 4.17 us
  between operations: 14.6 us -> 0.69 us
    pallas_call x0 -> x1, Pallas kernels: none -> 166 us  [local(): pl.pallas_call(step_kernel, out_shape=(jax.ShapeDtypeStruct((256, 1024),...]
    psum x1 -> x0, waiting for transfers between devices: 95.8 us -> none  [local(): total_sums, total_mass = lax.psum((top_sums, top_mass), ('dp', 'cent'))]
    psum x1 -> x0, blocking collectives: 65.2 us -> none  [local(): total_sums, total_mass = lax.psum((top_sums, top_mass), ('dp', 'cent'))]
    all_to_all x5 -> x0, waiting for transfers between devices: 64.2 us -> none  [the longest x1 39.7 us: local(): lax.all_to_all(outgoing, 'dp', split_axis=0, concat_axis=0, tiled=True)]
    dot_general x12 -> x0, matrix products: 63.5 us -> none  [the longest x4 33 us: rows_times(): lax.dot_general(left, right, (((1,), (1,)), ((), ())), preferred_element_...]
    reduce_scatter x1 -> x0, waiting for transfers between devices: 32.2 us -> none  [local(): lax.psum_scatter(group_sums, 'cent', scatter_dimension=0, tiled=True)]
    all_to_all x5 -> x0, starting transfers between devices: 28.9 us -> none  [the longest x1 10.3 us: local(): lax.all_to_all(row_peak.reshape(groups, CAP, block_rows), 'dp', split_axi...]
    reduce_sum x11 -> x2, other arithmetic: 26.8 us -> 0.28 us  [the longest x1 0.18 us: tables(): slot = targets * CAP + jnp.sum(earlier.astype(jnp.int32), 1)]
  transfers between devices with their start and end apart: 9 -> 0, of which waited for: 8 -> 0; matrix products, arithmetic and copies ran while one was open for 23% -> 0% of each run, Pallas kernels for 0% -> 0%
where the time goes in v1:
time: 172 us
  Pallas kernels  166 us (97%)
  local copies, waits for them, and re-layouts  4.17 us (2%)
    pallas_call x1, Pallas kernels, local(): pl.pallas_call(step_kernel, out_shape=(jax.ShapeDtypeStruct((256, 1024),...  166 us
    unnamed x7, local copies, waits for them, and re-layouts  3.65 us

profile of v1, /device:TPU:0, one launch (start us, length us, event | category | flops | bytes accessed | tf_op | source)
XLA Modules:
  0.0 171.9 jit_solution(3959940801884812929)
XLA Ops:
  0.6 0.0 copy-start.1
  0.7 0.1 pad.2.clone
  0.7 0.6 copy-done.1
  1.3 0.1 copy.10
  1.4 0.1 reshape.52
  1.5 0.2 convert_reduce_fusion
  1.7 0.1 slice.7
  1.8 0.1 slice.6
  1.9 0.1 copy.11
  2.0 0.1 add.34
  2.1 0.1 select_reduce_fusion.1
  2.2 0.7 add_add_fusion.table
  2.8 166.1 %lloyd_step.1 = (f32[256,1024]{1,0:T(8,128)}, f32[16,1024]{1,0:T(8,128)}) custom-call(bf16[8,2,32,1024]{3,2,1,0:T(8,128)(2,1)} %bitcast.6, bf16[256,1024]{1,0:T(8,128)(2,1)} %cen.1, s32[8,128]{1,0:T(8,128)} %add_add_fusion.table, bf16[16,1024]{1,0:T(8,128)(2,1)} %zin.1), custom_call_target="tpu_custom_call" | custom-call | tf_op jit(solution)/shard_map/lloyd_step/pallas_call | solution.py:462
  168.9 0.0 copy-start
  168.9 2.3 %copy.14 = f32[256,1024]{1,0:T(8,128)} copy(f32[256,1024]{1,0:T(8,128)} %get-tuple-element.8) | data formatting | bytes 2097152
  171.2 0.0 copy-done
  171.2 0.6 copy.15
  (4 shorter events, 0.0 us)
Async XLA Ops:
  0.6 0.7 copy-start.1
  168.9 2.4 %copy-start = (f32[16,1024]{1,0:T(8,128)S(1)}, f32[16,1024]{1,0:T(8,128)}, u32[]{:S(2)}) copy-start(f32[16,1024]{1,0:T(8,128)} %get-tuple-element.9) | copy-start | bytes 196612

commit v2 on v1

--- a/solution.py
+++ b/solution.py
@@ -11,11 +11,12 @@
 CAP = 2
 PRIOR = 1.0
 BIG = 1e5
+LIMIT = 32767.0
 F32 = jnp.float32
 BF16 = jnp.bfloat16
 PEERS = [(dy, dz) for dy in range(4) for dz in range(4) if (dy, dz) != (0, 0)]
-NEAR = [(dy, dz) for dy in (0, 1, 3) for dz in (0, 1, 3)]
-FAR = [(2, 0), (2, 1), (2, 2), (2, 3), (0, 2), (1, 2), (3, 2)]
+ORDER = [(0, 0), (0, 1), (1, 0), (0, 3), (3, 0), (1, 1), (1, 3), (3, 1), (3, 3)]
+ORDER += [(2, 0), (0, 2), (2, 1), (1, 2), (2, 3), (3, 2), (2, 2)]
 AXES_OF = ((2, 1, 0), (1, 0, 2), (0, 2, 1))
 
 
@@ -34,24 +35,30 @@
     return top + jnp.log(jnp.exp(a - top) + jnp.exp(b - top))
 
 
+def encode(value, code, scale, row):
+    peak = jnp.maximum(jnp.max(jnp.abs(value), 1, keepdims=True), 1e-30)
+    code[...] = jnp.round(value * (LIMIT / peak)).astype(jnp.int32).astype(jnp.int16)
+    wide = peak * (1.0 / LIMIT) + jnp.zeros((128, 128), F32)
+    scale[row:row + 1, :] = jnp.transpose(wide)[0:1, :]
+
+
+def decode(code, scale, row):
+    wide = jnp.transpose(scale[...])
+    return code[...].astype(jnp.int32).astype(F32) * wide[:, row:row + 1]
+
+
 def source_of(i):
-    j = i - 9
-    near_y, near_z = i // 3, i % 3
-    far_t = j - 4
-    dy = jnp.where(
-        i < 9, near_y + near_y // 2, jnp.where(j < 4, 2, far_t + far_t // 2)
-    )
-    dz = jnp.where(i < 9, near_z + near_z // 2, jnp.where(j < 4, j, 2))
-    return dy, dz
+    code = sum(jnp.where(i == n, dy * 4 + dz, 0) for n, (dy, dz) in enumerate(ORDER))
+    return code // 4, code % 4
 
 
 def step_kernel(
-    pts, cen, table, zin,
+    pts, cen, table, own, zin,
     one_out, two_out,
     tt, tt_sib, tts, zg1, zg2, zg3, yg1, yg2, yg3, outz, outy, x_all, c_all, sq, scores,
-    st, sto, stc, g_all, lse, w_buf, sums, sum_half, sum_full,
+    st, sto, stc, g_all, peaks, alpha, w_buf, sums, code_out, code_in, scale_out, scale_in,
     mass, mass_in, z_all, zsq, ch, stat, stat_in, wh, wl,
-    ha0, fu0, ha1, fu1, ha2, fu2,
+    t_code, t_code_in, t_scale, t_scale_in, ha1, fu1, ha2, fu2,
     ssem, rsem, lsem,
 ):
     dp = lax.axis_index("dp")
@@ -95,28 +102,22 @@
         pl.semaphore_signal(barrier, inc=1, device_id=at(**f), device_id_type=MESH)
     pl.semaphore_wait(barrier, len(friends))
 
+    t_near, t_far = [], []
+    for d in (1, 2, 3):
+        t_near.append(send(table, tt.at[dp], along(1, d)))
+        t_near.append(send(table, tt.at[dp], along(0, d)))
     z_one = {d: send(pts.at[:, 0], zg[d], along(1, d)) for d in (1, 3)}
     y_one = {d: send(pts.at[:, 1], yg[d], along(0, d)) for d in (1, 3)}
     c_one = {d: send(cen, c_all.at[d], along(2, d)) for d in (1, 3)}
-    t_copy = {
-        (a, b): send(table, tt.at[dp], at(dy=a, dz=b)) for a, b in PEERS
-    }
-    zx = {d: send(zin, z_all.at[0, 0, d], along(2, d)) for d in (1, 2, 3)}
     tt[dp] = table[...]
     c_all[0] = cen[...]
     z_all[0, 0, 0] = zin[...]
-    for t in t_copy.values():
-        t.wait_recv()
-    tt_copy = send(tt, tt_sib, at(dc=1))
-    local = pltpu.make_async_copy(tt, tts, lsem.at[0])
-    local.start()
-    local.wait()
 
     arrive = {}
 
     def slots(r):
-        from_z = tts.at[y * 4 + (z - r) % 4]
-        from_y = tts.at[((y - r) % 4) * 4 + z]
+        from_z = own if r == 0 else tts.at[y * 4 + (z - r) % 4]
+        from_y = own if r == 0 else tts.at[((y - r) % 4) * 4 + z]
         for d in (2, 1, 3, 0):
             for k in range(2):
                 group = ((y + d) % 4) * 4 + z
@@ -142,6 +143,16 @@
                 )
 
     slots(0)
+    for a, b in PEERS:
+        if a and b:
+            t_far.append(send(table, tt.at[dp], at(dy=a, dz=b)))
+    zx = {d: send(zin, z_all.at[0, 0, d], along(2, d)) for d in (1, 2, 3)}
+    for t in t_near + t_far:
+        t.wait_recv()
+    tt_copy = send(tt, tt_sib, at(dc=1))
+    local = pltpu.make_async_copy(tt, tts, lsem.at[0])
+    local.start()
+    local.wait()
     z_one[1].wait_recv()
     z_fwd = [send(zg[1].at[0:4], zg[2].at[0:4], along(1, 1))]
     y_one[1].wait_recv()
@@ -176,9 +187,11 @@
         product = nt(c_all[...].reshape(1024, 1024), rows)
         for k in range(2):
             half = product[:, k * 128:(k + 1) * 128] * (1.0 / 32.0) - sq[...]
-            scores[s * 2 + k] = half.reshape(4, 4, 4, 16, 128)
             peak = jnp.max(half, 0, keepdims=True)
-            total = jnp.sum(jnp.exp(half - peak), 0, keepdims=True)
+            raised = jnp.exp(half - peak)
+            scores[s * 2 + k] = raised.reshape(4, 4, 4, 16, 128)
+            total = jnp.sum(raised, 0, keepdims=True)
+            peaks[k, pl.ds(s_abs, 1), :] = peak
             st[k, pl.ds(s_abs, 1), :] = peak + jnp.log(total)
         return carry
 
@@ -193,14 +206,22 @@
                 arrive[dy, dz, 1].wait_recv()
             sib[dy, dz] = send(x_all.at[s, :, c], x_all.at[s, :, c], at(dc=1))
 
-    forward(NEAR)
-    for p in NEAR:
-        sib[p].wait_recv()
-    lax.fori_loop(0, 9, score_chunk, 0)
-    forward(FAR)
-    for p in FAR:
-        sib[p].wait_recv()
-    lax.fori_loop(9, 16, score_chunk, 0)
+    def score(lo, hi):
+        for p in ORDER[lo:hi]:
+            sib[p].wait_recv()
+        lax.fori_loop(lo, hi, score_chunk, 0)
+
+    forward(ORDER[0:5])
+    forward(ORDER[5:9])
+    score(0, 5)
+    forward(ORDER[9:11])
+    score(5, 9)
+    forward(ORDER[11:15])
+    score(9, 11)
+    score(11, 14)
+    forward(ORDER[15:])
+    score(14, 15)
+    score(15, 16)
 
     st_copy = send(st, sto, at(dc=1))
     st_copy.wait_recv()
@@ -229,7 +250,8 @@
         return jnp.where(slot >= 0.0, log_add(stc[k], other), BIG)
 
     for k in range(2):
-        lse[k] = jnp.where(mine, other_group(tt, k), other_group(tt_sib, k))
+        total = jnp.where(mine, other_group(tt, k), other_group(tt_sib, k))
+        alpha[k] = jnp.exp(peaks[k] - total)
 
     def weigh(r):
         def one(s, carry):
@@ -237,9 +259,9 @@
             s_abs = ((y - dy) % 4) * 4 + (z - dz) % 4
             for k in range(2):
                 col = pl.multiple_of(s * 256 + k * 128, 128)
-                row = lse[k, pl.ds(s_abs, 1), :]
-                w_buf[:, pl.ds(col, 128)] = jnp.exp(
-                    scores[s * 2 + k, r].reshape(256, 128) - row
+                row = alpha[k, pl.ds(s_abs, 1), :]
+                w_buf[:, pl.ds(col, 128)] = (
+                    scores[s * 2 + k, r].reshape(256, 128) * row
                 ).astype(BF16)
             return carry
 
@@ -254,28 +276,37 @@
 
         lax.fori_loop(0, 4, tile, 0)
 
-    lo, hi = pl.ds(0, 128), pl.ds(128, 128)
+    lo, hi = slice(0, 128), slice(128, 256)
+
+    def push(n, value, d):
+        encode(value, code_out.at[n], scale_out.at[n], 0)
+        return (
+            send(code_out.at[n], code_in.at[n], along(2, d)),
+            send(scale_out.at[n], scale_in.at[n], along(2, d)),
+        )
+
+    def pull(n, copies):
+        for copy in copies:
+            copy.wait_recv()
+        return decode(code_in.at[n], scale_in.at[n], 0)
+
     weigh(2)
-    via_a = send(sums.at[2, lo], sum_half.at[0], along(2, 1))
-    via_b = send(sums.at[2, hi], sum_half.at[1], along(2, 3))
+    via_a = push(0, sums[2, lo], 1)
+    via_b = push(1, sums[2, hi], 3)
     mass_a = send(mass.at[2], mass_in.at[0], along(2, 1))
     for copy in zz:
         copy.wait_recv()
     zy = [send(z_all.at[0], z_all.at[d], along(0, d)) for d in (1, 2, 3)]
     weigh(3)
-    last = [send(sums.at[3, hi], sum_full.at[0, hi], along(2, 1))]
+    up_hi = push(3, sums[3, hi], 1)
     weigh(1)
-    last.append(send(sums.at[1, lo], sum_full.at[1, lo], along(2, 3)))
-    last.append(send(mass.at[1], mass_in.at[2], along(2, 3)))
-    via_a.wait_recv()
-    sums[3, lo] += sum_half[0]
-    last.append(send(sums.at[3, lo], sum_full.at[0, lo], along(2, 1)))
+    down_lo = push(4, sums[1, lo], 3)
+    mass_down = send(mass.at[1], mass_in.at[2], along(2, 3))
+    up_lo = push(2, sums[3, lo] + pull(0, via_a), 1)
     mass_a.wait_recv()
     mass[3] += mass_in[0]
-    last.append(send(mass.at[3], mass_in.at[1], along(2, 1)))
-    via_b.wait_recv()
-    sums[1, hi] += sum_half[1]
-    last.append(send(sums.at[1, hi], sum_full.at[1, hi], along(2, 3)))
+    mass_up = send(mass.at[3], mass_in.at[1], along(2, 1))
+    down_hi = push(5, sums[1, hi] + pull(1, via_b), 3)
     weigh(0)
     for copy in zy:
         copy.wait_recv()
@@ -285,11 +316,17 @@
         ) * (1.0 / 16.0)
         + jnp.zeros((1024, 128), F32)
     )
-    for copy in last:
-        copy.wait_recv()
+    mass_down.wait_recv()
+    mass_up.wait_recv()
     own_mass = jnp.transpose(mass[0] + mass_in[1] + mass_in[2])[:, 0:1]
-    own_sums = sums[0] + sum_full[0] + sum_full[1]
-    one_out[...] = (own_sums + PRIOR * cen[...].astype(F32)) / (own_mass + PRIOR)
+    for rows, above, n_above, below, n_below in (
+        (hi, up_hi, 3, down_hi, 5),
+        (lo, up_lo, 2, down_lo, 4),
+    ):
+        total = sums[0, rows] + pull(n_above, above) + pull(n_below, below)
+        one_out[rows] = (total + PRIOR * cen[rows].astype(F32)) / (
+            own_mass[rows] + PRIOR
+        )
 
     ch[0, 0] = one_out[...].astype(BF16)
     ch[0, 1] = (one_out[...] - ch[0, 0].astype(F32)).astype(BF16)
@@ -301,10 +338,11 @@
         for k in range(2):
             cols = slice(k * 128, (k + 1) * 128)
             half = product[:, cols] * (1.0 / 8.0) - zsq[...]
-            scores[16 + h * 2 + k] = half.reshape(4, 4, 4, 16, 128)
             peak = jnp.max(half, 0, keepdims=True)
+            raised = jnp.exp(half - peak)
+            scores[16 + h * 2 + k] = raised.reshape(4, 4, 4, 16, 128)
             stat[h, 0:1, cols] = peak
-            stat[h, 1:2, cols] = jnp.sum(jnp.exp(half - peak), 0, keepdims=True)
+            stat[h, 1:2, cols] = jnp.sum(raised, 0, keepdims=True)
         return carry
 
     lax.fori_loop(0, 1, top_scores, 0)
@@ -315,15 +353,15 @@
     mass_two = jnp.zeros((1024, 1), F32)
     for h in range(2):
         peak = jnp.maximum(stat[h, 0:1], stat_in[1 - h, 0:1])
-        total = stat[h, 1:2] * jnp.exp(stat[h, 0:1] - peak) + stat_in[
-            1 - h, 1:2
-        ] * jnp.exp(stat_in[1 - h, 0:1] - peak)
-        scale = 1.0 / total
+        mine_up = jnp.exp(stat[h, 0:1] - peak)
+        total = stat[h, 1:2] * mine_up + stat_in[1 - h, 1:2] * jnp.exp(
+            stat_in[1 - h, 0:1] - peak
+        )
+        scale = mine_up / total
         for k in range(2):
             part = slice(k * 128, (k + 1) * 128)
             weight = (
-                jnp.exp(scores[16 + h * 2 + k].reshape(1024, 128) - peak[:, part])
-                * scale[:, part]
+                scores[16 + h * 2 + k].reshape(1024, 128) * scale[:, part]
             )
             cols = slice(h * 256 + k * 128, h * 256 + (k + 1) * 128)
             wh[:, cols] = weight.astype(BF16)
@@ -338,8 +376,8 @@
             scores[q * 2 + k] = part[:, k * 128:(k + 1) * 128].reshape(4, 4, 4, 16, 128)
     scores[8] = (mass_two + jnp.zeros((1024, 128), F32)).reshape(4, 4, 4, 16, 128)
 
-    halves = (ha0, ha1, ha2)
-    fulls = (fu0, fu1, fu2)
+    halves = (None, ha1, ha2)
+    fulls = (None, fu1, fu2)
 
     def chunk(q, stage, r, half=None):
         where = [slice(None)] * 3
@@ -358,7 +396,40 @@
         size = 2 if stage < 2 else 8
         return ref.at[:, pl.ds(half * size, size)]
 
-    for stage in range(3):
+    def top_push(q, n, r, half, d):
+        axis = AXES_OF[q][0]
+        value = chunk(q, 0, r, half)[...].reshape(3, 128, 128)
+        for b in range(3):
+            encode(value[b], t_code.at[q, n, b], t_scale.at[q, n], b)
+        return (
+            send(t_code.at[q, n], t_code_in.at[q, n], along(axis, d)),
+            send(t_scale.at[q, n], t_scale_in.at[q, n], along(axis, d)),
+        )
+
+    def top_pull(q, n, copies, r, half):
+        for copy in copies:
+            copy.wait_recv()
+        view = chunk(q, 0, r, half)
+        parts = [
+            decode(t_code_in.at[q, n, b], t_scale_in.at[q, n], b)[None] for b in range(3)
+        ]
+        view[...] += jnp.concatenate(parts, 0).reshape(view.shape)
+
+    via = [(top_push(q, 0, 2, 0, 1), top_push(q, 1, 2, 1, 3)) for q in range(3)]
+    early = [(top_push(q, 3, 3, 1, 1), top_push(q, 4, 1, 0, 3)) for q in range(3)]
+    late = []
+    for q in range(3):
+        top_pull(q, 0, via[q][0], 3, 0)
+        up = top_push(q, 2, 3, 0, 1)
+        top_pull(q, 1, via[q][1], 1, 1)
+        late.append((up, top_push(q, 5, 1, 1, 3)))
+    for q in range(3):
+        top_pull(q, 3, early[q][0], 0, 1)
+        top_pull(q, 4, early[q][1], 0, 0)
+        top_pull(q, 2, late[q][0], 0, 0)
+        top_pull(q, 5, late[q][1], 0, 1)
+
+    for stage in range(1, 3):
         ha, fu = halves[stage], fulls[stage]
         first, second = {}, {}
         for q in range(3):
@@ -394,6 +465,7 @@
         two_out[:, cols] = (
             scores[q, 0, 0, 0] + PRIOR * zin[:, cols].astype(F32)
         ) / denominator
+    assert counter[0] <= ssem.shape[0]
     for copy in sent:
         copy.wait_send()
 
@@ -417,7 +489,7 @@
 
 def local(points, candidates, level_one, level_two):
     vmem = pl.BlockSpec(memory_space=pltpu.VMEM)
-    n_copies = 158
+    n_copies = 190
     dma = pltpu.SemaphoreType.DMA
     scratch = [
         pltpu.VMEM((16, 8, 128), jnp.int32),
@@ -436,10 +508,11 @@
         pltpu.VMEM((2, 16, 128), F32),
         pltpu.VMEM((16, 2, 16, 128), F32),
         pltpu.VMEM((2, 16, 128), F32),
+        pltpu.VMEM((2, 16, 128), F32),
         pltpu.VMEM((256, 4096), BF16),
         pltpu.VMEM((4, 256, 1024), F32),
-        pltpu.VMEM((2, 128, 1024), F32),
-        pltpu.VMEM((2, 256, 1024), F32),
+        *[pltpu.VMEM((6, 128, 1024), jnp.int16)] * 2,
+        *[pltpu.VMEM((6, 8, 128), F32)] * 2,
         pltpu.VMEM((4, 8, 256), F32),
         pltpu.VMEM((3, 8, 256), F32),
         pltpu.VMEM((4, 4, 4, 16, 1024), BF16),
@@ -449,8 +522,8 @@
         pltpu.VMEM((2, 8, 256), F32),
         pltpu.VMEM((1024, 512), BF16),
         pltpu.VMEM((1024, 512), BF16),
-        pltpu.VMEM((3, 2, 3, 2, 4, 16, 128), F32),
-        pltpu.VMEM((3, 2, 3, 4, 4, 16, 128), F32),
+        *[pltpu.VMEM((3, 6, 3, 128, 128), jnp.int16)] * 2,
+        *[pltpu.VMEM((3, 6, 8, 128), F32)] * 2,
         pltpu.VMEM((3, 2, 3, 2, 16, 128), F32),
         pltpu.VMEM((3, 2, 3, 4, 16, 128), F32),
         pltpu.VMEM((3, 2, 3, 8, 128), F32),
@@ -459,20 +532,21 @@
         dma((n_copies,)),
         dma((1,)),
     ]
+    table = tables(candidates)
     return pl.pallas_call(
         step_kernel,
         out_shape=(
             jax.ShapeDtypeStruct((256, 1024), F32),
             jax.ShapeDtypeStruct((16, 1024), F32),
         ),
-        in_specs=[vmem] * 4,
+        in_specs=[vmem, vmem, vmem, pl.BlockSpec(memory_space=pltpu.SMEM), vmem],
         out_specs=(vmem, vmem),
         scratch_shapes=scratch,
         compiler_params=pltpu.CompilerParams(
             collective_id=0, has_side_effects=True, vmem_limit_bytes=62 * 2**20
         ),
         name="lloyd_step",
-    )(points.reshape(8, 2, 32, 1024), level_one, tables(candidates), level_two)
+    )(points.reshape(8, 2, 32, 1024), level_one, table, table, level_two)
 
 
 def solution(mesh):

time: 172 us -> 159 us (0.924)
  Pallas kernels: 166 us -> 153 us
    pallas_call x1, Pallas kernels: 166 us -> 153 us  [local(): pl.pallas_call(step_kernel, out_shape=(jax.ShapeDtypeStruct((256, 1024),...]
where the time goes in v2:
time: 159 us
  Pallas kernels  153 us (96%)
  local copies, waits for them, and re-layouts  4.17 us (3%)
    pallas_call x1, Pallas kernels, local(): pl.pallas_call(step_kernel, out_shape=(jax.ShapeDtypeStruct((256, 1024),...  153 us
    unnamed x7, local copies, waits for them, and re-layouts  3.65 us

profile of v2, /device:TPU:0, one launch (start us, length us, event | category | flops | bytes accessed | tf_op | source)
XLA Modules:
  0.0 159.0 jit_solution(4944220758696708050)
XLA Ops:
  0.6 0.0 copy-start.1
  0.7 0.1 pad.2.clone
  0.7 0.6 copy-done.1
  1.3 0.1 copy.10
  1.4 0.1 reshape.52
  1.5 0.2 convert_reduce_fusion
  1.7 0.1 slice.7
  1.8 0.1 slice.6
  1.9 0.1 copy.11
  2.0 0.1 add.34
  2.1 0.1 select_reduce_fusion.1
  2.2 0.7 add_add_fusion.table.own
  2.8 153.2 %lloyd_step.1 = (f32[256,1024]{1,0:T(8,128)}, f32[16,1024]{1,0:T(8,128)}) custom-call(bf16[8,2,32,1024]{3,2,1,0:T(8,128)(2,1)} %bitcast.6, bf16[256,1024]{1,0:T(8,128)(2,1)} %cen.1, s32[8,128]{1,0:T(8,128)} %add_add_fusion.table.own, s32[8,128]{1,0:T(8,128)} %add_add_fusion.table.own, bf16[16,1024]{1,0:T(8,128)(2,1)} %zin.1), custom_call_target="tpu_custom_call" | custom-call | tf_op jit(solution)/shard_map/lloyd_step/pallas_call | solution.py:536
  156.0 0.0 copy-start
  156.0 2.3 %copy.14 = f32[256,1024]{1,0:T(8,128)} copy(f32[256,1024]{1,0:T(8,128)} %get-tuple-element.8) | data formatting | bytes 2097152
  158.4 0.0 copy-done
  158.4 0.6 copy.15
  (4 shorter events, 0.0 us)
Async XLA Ops:
  0.6 0.7 copy-start.1
  156.0 2.4 %copy-start = (f32[16,1024]{1,0:T(8,128)S(1)}, f32[16,1024]{1,0:T(8,128)}, u32[]{:S(2)}) copy-start(f32[16,1024]{1,0:T(8,128)} %get-tuple-element.9) | copy-start | bytes 196612

commit v3 on v2

--- a/solution.py
+++ b/solution.py
@@ -35,16 +35,22 @@
     return top + jnp.log(jnp.exp(a - top) + jnp.exp(b - top))
 
 
-def encode(value, code, scale, row):
-    peak = jnp.maximum(jnp.max(jnp.abs(value), 1, keepdims=True), 1e-30)
-    code[...] = jnp.round(value * (LIMIT / peak)).astype(jnp.int32).astype(jnp.int16)
-    wide = peak * (1.0 / LIMIT) + jnp.zeros((128, 128), F32)
-    scale[row:row + 1, :] = jnp.transpose(wide)[0:1, :]
-
-
-def decode(code, scale, row):
+def encode(values, codes, scale):
+    lane = lax.broadcasted_iota(jnp.int32, (128, 128), 1)
+    wide = jnp.zeros((128, 128), F32)
+    for n, (value, code) in enumerate(zip(values, codes)):
+        peak = jnp.maximum(jnp.max(jnp.abs(value), 1, keepdims=True), 1e-30)
+        code[...] = jnp.round(value * (LIMIT / peak)).astype(jnp.int32).astype(jnp.int16)
+        wide = jnp.where(lane == n, peak * (1.0 / LIMIT), wide)
+    scale[...] = jnp.transpose(wide)[0:8, :]
+
+
+def decode(codes, scale):
     wide = jnp.transpose(scale[...])
-    return code[...].astype(jnp.int32).astype(F32) * wide[:, row:row + 1]
+    return [
+        code[...].astype(jnp.int32).astype(F32) * wide[:, n:n + 1]
+        for n, code in enumerate(codes)
+    ]
 
 
 def source_of(i):
@@ -54,7 +60,7 @@
 
 def step_kernel(
     pts, cen, table, own, zin,
-    one_out, two_out,
+    one_out, den_out, two_out,
     tt, tt_sib, tts, zg1, zg2, zg3, yg1, yg2, yg3, outz, outy, x_all, c_all, sq, scores,
     st, sto, stc, g_all, peaks, alpha, w_buf, sums, code_out, code_in, scale_out, scale_in,
     mass, mass_in, z_all, zsq, ch, stat, stat_in, wh, wl,
@@ -279,7 +285,7 @@
     lo, hi = slice(0, 128), slice(128, 256)
 
     def push(n, value, d):
-        encode(value, code_out.at[n], scale_out.at[n], 0)
+        encode([value], [code_out.at[n]], scale_out.at[n])
         return (
             send(code_out.at[n], code_in.at[n], along(2, d)),
             send(scale_out.at[n], scale_in.at[n], along(2, d)),
@@ -288,7 +294,7 @@
     def pull(n, copies):
         for copy in copies:
             copy.wait_recv()
-        return decode(code_in.at[n], scale_in.at[n], 0)
+        return decode([code_in.at[n]], scale_in.at[n])[0]
 
     weigh(2)
     via_a = push(0, sums[2, lo], 1)
@@ -324,12 +330,14 @@
         (lo, up_lo, 2, down_lo, 4),
     ):
         total = sums[0, rows] + pull(n_above, above) + pull(n_below, below)
-        one_out[rows] = (total + PRIOR * cen[rows].astype(F32)) / (
-            own_mass[rows] + PRIOR
-        )
-
-    ch[0, 0] = one_out[...].astype(BF16)
-    ch[0, 1] = (one_out[...] - ch[0, 0].astype(F32)).astype(BF16)
+        above_line = total + PRIOR * cen[rows].astype(F32)
+        below_line = own_mass[rows] + PRIOR
+        one_out[rows] = above_line
+        den_out[rows] = below_line + jnp.zeros((128, 128), F32)
+        value = above_line / below_line
+        ch[0, 0, rows] = value.astype(BF16)
+        ch[0, 1, rows] = (value - ch[0, 0, rows].astype(F32)).astype(BF16)
+
     ch_copy = send(ch.at[0], ch.at[1], at(dc=1))
 
     def top_scores(h, carry):
@@ -367,14 +375,18 @@
             wh[:, cols] = weight.astype(BF16)
             wl[:, cols] = (weight - wh[:, cols].astype(F32)).astype(BF16)
             mass_two = mass_two + jnp.sum(weight, 1, keepdims=True)
-    for q in range(4):
-        cols = slice(q * 256, (q + 1) * 256)
-        hi_rows = ch[:, 0, :, cols].reshape(512, 256)
-        lo_rows = ch[:, 1, :, cols].reshape(512, 256)
+    def top_part(q):
+        width = 384 if q < 2 else 256
+        cols = slice(q * 384, q * 384 + width)
+        hi_rows = ch[:, 0, :, cols].reshape(512, width)
+        lo_rows = ch[:, 1, :, cols].reshape(512, width)
         part = nn(wh[...], hi_rows) + nn(wl[...], hi_rows) + nn(wh[...], lo_rows)
-        for k in range(2):
-            scores[q * 2 + k] = part[:, k * 128:(k + 1) * 128].reshape(4, 4, 4, 16, 128)
-    scores[8] = (mass_two + jnp.zeros((1024, 128), F32)).reshape(4, 4, 4, 16, 128)
+        for k in range(width // 128):
+            scores[q * 3 + k] = part[:, k * 128:(k + 1) * 128].reshape(4, 4, 4, 16, 128)
+        if q == 2:
+            scores[8] = (mass_two + jnp.zeros((1024, 128), F32)).reshape(
+                4, 4, 4, 16, 128
+            )
 
     halves = (None, ha1, ha2)
     fulls = (None, fu1, fu2)
@@ -399,8 +411,11 @@
     def top_push(q, n, r, half, d):
         axis = AXES_OF[q][0]
         value = chunk(q, 0, r, half)[...].reshape(3, 128, 128)
-        for b in range(3):
-            encode(value[b], t_code.at[q, n, b], t_scale.at[q, n], b)
+        encode(
+            [value[b] for b in range(3)],
+            [t_code.at[q, n, b] for b in range(3)],
+            t_scale.at[q, n],
+        )
         return (
             send(t_code.at[q, n], t_code_in.at[q, n], along(axis, d)),
             send(t_scale.at[q, n], t_scale_in.at[q, n], along(axis, d)),
@@ -410,12 +425,16 @@
         for copy in copies:
             copy.wait_recv()
         view = chunk(q, 0, r, half)
-        parts = [
-            decode(t_code_in.at[q, n, b], t_scale_in.at[q, n], b)[None] for b in range(3)
-        ]
-        view[...] += jnp.concatenate(parts, 0).reshape(view.shape)
-
-    via = [(top_push(q, 0, 2, 0, 1), top_push(q, 1, 2, 1, 3)) for q in range(3)]
+        parts = decode(
+            [t_code_in.at[q, n, b] for b in range(3)], t_scale_in.at[q, n]
+        )
+        view[...] += jnp.stack(parts, 0).reshape(view.shape)
+
+    via = []
+    for q in (2, 0, 1):
+        top_part(q)
+        via.append((q, (top_push(q, 0, 2, 0, 1), top_push(q, 1, 2, 1, 3))))
+    via = dict(via)
     early = [(top_push(q, 3, 3, 1, 1), top_push(q, 4, 1, 0, 3)) for q in range(3)]
     late = []
     for q in range(3):
@@ -533,20 +552,22 @@
         dma((1,)),
     ]
     table = tables(candidates)
-    return pl.pallas_call(
+    one, den, two = pl.pallas_call(
         step_kernel,
         out_shape=(
             jax.ShapeDtypeStruct((256, 1024), F32),
+            jax.ShapeDtypeStruct((256, 128), F32),
             jax.ShapeDtypeStruct((16, 1024), F32),
         ),
         in_specs=[vmem, vmem, vmem, pl.BlockSpec(memory_space=pltpu.SMEM), vmem],
-        out_specs=(vmem, vmem),
+        out_specs=(vmem, vmem, vmem),
         scratch_shapes=scratch,
         compiler_params=pltpu.CompilerParams(
             collective_id=0, has_side_effects=True, vmem_limit_bytes=62 * 2**20
         ),
         name="lloyd_step",
     )(points.reshape(8, 2, 32, 1024), level_one, table, table, level_two)
+    return one / den[:, 0:1], two
 
 
 def solution(mesh):

time: 159 us -> 164 us (1.031)
  Pallas kernels: 153 us -> 157 us
  other arithmetic: 0.97 us -> 3.35 us
    pallas_call x1, Pallas kernels: 153 us -> 157 us  [local(): pl.pallas_call(step_kernel, out_shape=(jax.ShapeDtypeStruct((256, 1024),...]
    div x0 -> x1, other arithmetic: none -> 2.38 us  [local(): return (one / den[:, 0:1], two)]
    unnamed x7 -> x6, local copies, waits for them, and re-layouts: 3.65 us -> 1.31 us
where the time goes in v3:
time: 164 us
  Pallas kernels  157 us (96%)
  other arithmetic  3.35 us (2%)
  local copies, waits for them, and re-layouts  2.83 us (2%)
    pallas_call x1, Pallas kernels, local(): pl.pallas_call(step_kernel, out_shape=(jax.ShapeDtypeStruct((256, 1024),...  157 us

profile of v3, /device:TPU:0, one launch (start us, length us, event | category | flops | bytes accessed | tf_op | source)
XLA Modules:
  0.0 164.2 jit_solution(2702090943732820907)
XLA Ops:
  0.6 0.0 copy-start.1
  0.7 0.1 pad.2.clone
  0.7 0.6 copy-done.1
  1.3 0.1 copy.10
  1.4 0.1 reshape.52
  1.5 0.2 convert_reduce_fusion
  1.7 0.1 slice.10
  1.8 0.1 slice.9
  1.9 0.1 copy.11
  2.0 0.1 add.34
  2.1 0.1 select_reduce_fusion.1
  2.2 0.7 add_add_fusion.table.own
  2.8 157.4 %lloyd_step.1 = (f32[256,1024]{1,0:T(8,128)}, f32[256,128]{1,0:T(8,128)}, f32[16,1024]{1,0:T(8,128)}) custom-call(bf16[8,2,32,1024]{3,2,1,0:T(8,128)(2,1)} %bitcast.6, bf16[256,1024]{1,0:T(8,128)(2,1)} %cen.1, s32[8,128]{1,0:T(8,128)} %add_add_fusion.table.own, s32[8,128]{1,0:T(8,128)} %add_add_fusion.table.own, bf16[16,1024]{1,0:T(8,128)(2,1)} %zin.1), custom_call_target="tpu_custom_call" | custom-call | tf_op jit(solution)/shard_map/lloyd_step/pallas_call | solution.py:555
  160.2 1.0 slice_reduce_fusion
  161.2 0.0 copy-start
  161.2 2.4 %broadcast_divide_fusion = f32[256,1024]{1,0:T(8,128)} fusion(f32[256,1024]{1,0:T(8,128)} %get-tuple-element.5, f32[256]{0:T(256)S(1)} %slice_reduce_fusion), kind=kLoop, calls=%fused_computation | loop fusion | flops 262144 | bytes 2098176 | tf_op jit(solution)/shard_map/div | solution.py:570
  163.6 0.0 copy-done
  163.6 0.6 copy.13
  (4 shorter events, 0.0 us)
Async XLA Ops:
  0.6 0.7 copy-start.1
  161.2 2.4 %copy-start = (f32[16,1024]{1,0:T(8,128)S(1)}, f32[16,1024]{1,0:T(8,128)}, u32[]{:S(2)}) copy-start(f32[16,1024]{1,0:T(8,128)} %get-tuple-element.15) | copy-start | bytes 196612
